TPU v7x, 512 devices: a whole 4x4x16 slice. The times are simulated.
512 devices in a mesh: segment: 8 (over y, core), expert: 64 (over x, z).
Axes of the slice: x: 4, y: 4, z: 16, core: 2. Of those that a mesh axis runs over, the one named last changes fastest.
Arguments:
- hidden: bfloat16 [8, 2048, 2048], P('segment', 'expert'), may hold values from -6 to 6
- memory: bfloat16 [8, 2048, 2048], P('segment', 'expert'), may hold values from -6 to 6
- lengths: int32 [8, 64], P('segment', 'expert'), may hold values from 1 to 32, as said below
- memory_lengths: int32 [8, 64], P('segment', 'expert'), may hold values from 1 to 32, as said below
- routes: int32 [8, 2048, 2], P('segment', 'expert'), may hold values from 0 to 3, all different within a row; in each aligned block of 32 rows (0 to 31, 32 to 63, ..., all dimensions but the last counted through in order) at most 20 rows name the same one
- norm_gain: float32 [8, 3, 2048], P('segment'), may hold values from 0.5 to 1.5, as said below
- router: bfloat16 [8, 2048, 4], P('segment'), may hold values from -0.26516504 to 0.26516504, as said below
- w_in: bfloat16 [8, 2048, 16384], P('segment', None, 'expert'), may hold values from -0.13258252 to 0.13258252, as said below
- w_out: bfloat16 [8, 16384, 2048], P('segment', 'expert'), may hold values from -0.125 to 0.125, as said below
- shortlist: bfloat16 [8, 2048, 512], P('segment'), may hold values from -0.375 to 0.375
- student: float32 [8, 2048, 512], P('segment', 'expert'), may hold values from -15 to 15
- targets: int32 [8, 2048], P('segment', 'expert'), may hold values from 0 to 511
Outputs:
- layer_out: bfloat16 [8, 2048, 2048], P('segment', 'expert')
- loss: float32 [], replicated
Inputs may be any that keep to these rules, and one draw needn't show every extreme that they name: `lengths`: every sequence has at least one position; the first sequence of each section has 32. `memory_lengths`: every sequence has at least one position; the first sequence of each section has 32. `routes`: A token's two experts differ. In the 32 rows of one device no expert is named more than 20 times, a bound that some block reaches. `norm_gain`: equal in all encoder sections, and equal in all decoder sections. `router`: equal in all encoder sections, and equal in all decoder sections. `w_in`: equal in all encoder sections, and equal in all decoder sections. `w_out`: equal in all encoder sections, and equal in all decoder sections.
All inputs are finite; a program needn't handle non-finite values.
Results may differ from a plain program's by a relative error of at most 0.0049.
Values may be sent and summed in bfloat16 or wider, within the bound.
No kernel may reach another device: no remote copies, remote signals or barrier semaphores. Data moves between devices by JAX's collectives and lax.ppermute only.
A program may use at most 64 MiB of HBM per device.

v0:
```python
import math
import jax
import jax.numpy as jnp
from jax import lax
from jax.sharding import Mesh, PartitionSpec as P

HEADS = 16
HEAD_DIM = 128
LEN = 32
epsilon = 1e-05


def passed_along(block, axis, distance):
    devices = range(lax.axis_size(axis))
    route = [(i - distance, i) for i in devices if i - distance in devices]
    return lax.ppermute(block, axis, route)


def layer_norm(values, gain_row):
    centred = values - jnp.mean(values, axis=-1, keepdims=True)
    spread = jnp.mean(centred * centred, axis=-1, keepdims=True)
    return centred * lax.rsqrt(spread + epsilon) * gain_row


def expert_rows(rows, first_weight, second_weight):
    activated = jnp.maximum(
        jnp.dot(rows, first_weight, preferred_element_type=jnp.float32), 0.0
    ).astype(jnp.bfloat16)
    return jnp.dot(activated, second_weight, preferred_element_type=jnp.float32).astype(
        jnp.bfloat16
    )


def local(
    hidden,
    memory,
    lengths,
    memory_lengths,
    routes,
    norm_gain,
    router,
    w_in,
    w_out,
    shortlist,
    student,
    targets,
):
    chips = lax.axis_size("y")
    experts = router.shape[2]
    tok_rows = hidden.shape[1]
    model_width = hidden.shape[2]
    capacity = 5 * tok_rows // 8
    decoder = lax.axis_index("y") >= chips // 2
    positions = jnp.arange(tok_rows) % LEN
    seq_index = jnp.arange(tok_rows) // LEN
    is_valid = positions < lengths[0][seq_index]
    key_mask = (positions < memory_lengths[0][seq_index]).astype(jnp.bfloat16)
    arrived, arrived_mask = passed_along((memory[0], key_mask), "y", chips // 2)
    states = hidden[0].astype(jnp.float32)
    gain_rows = norm_gain[0]
    seq_count = tok_rows // LEN
    score_scale = 1.0 / math.sqrt(HEAD_DIM)
    queries = (
        layer_norm(states, gain_rows[0])
        .astype(jnp.bfloat16)
        .reshape(seq_count, LEN, HEADS, HEAD_DIM)
    )
    key_rows = arrived.reshape(seq_count, LEN, HEADS, HEAD_DIM)
    scores = (
        jnp.einsum("bqhd,bkhd->bhqk", queries, key_rows, preferred_element_type=jnp.float32)
        * score_scale
    )
    allowed = arrived_mask.reshape(seq_count, 1, 1, LEN) > 0.5
    scores = jnp.where(allowed, scores, -1e30)
    weights = jax.nn.softmax(scores, axis=-1).astype(jnp.bfloat16)
    attended = jnp.einsum(
        "bhqk,bkhd->bqhd", weights, key_rows, preferred_element_type=jnp.float32
    ).reshape(tok_rows, model_width)
    mid_states = states + jnp.where(decoder, attended, 0.0)
    normed = layer_norm(mid_states, gain_rows[1]).astype(jnp.bfloat16)
    router_probs = jax.nn.softmax(
        jnp.dot(normed, router[0], preferred_element_type=jnp.float32), axis=-1
    )
    expert_ids = jnp.arange(experts)
    first_hot = (routes[0][:, 0:1] == expert_ids).astype(jnp.float32)
    second = (routes[0][:, 1:2] == expert_ids).astype(jnp.float32)
    prob_first = jnp.sum(router_probs * first_hot, axis=-1, keepdims=True)
    prob_second = jnp.sum(router_probs * second, axis=-1, keepdims=True)
    prob_total = prob_first + prob_second
    gate_rows = (prob_first * first_hot + prob_second * second) / prob_total
    chosen = (first_hot + second) * is_valid[:, None].astype(jnp.float32)
    upto = (jnp.arange(tok_rows)[:, None] >= jnp.arange(tok_rows)[None, :]).astype(jnp.float32)
    slot_rank = jnp.dot(upto, chosen, preferred_element_type=jnp.float32) - 1.0
    slot_ids = jnp.arange(capacity).astype(jnp.float32)
    placing = chosen.T[:, None, :] * (slot_rank.T[:, None, :] == slot_ids[None, :, None]).astype(
        jnp.float32
    )
    buffer = jnp.einsum(
        "ect,td->ecd", placing.astype(jnp.bfloat16), normed, preferred_element_type=jnp.float32
    ).astype(jnp.bfloat16)
    at_expert = lax.all_to_all(buffer, "x", split_axis=0, concat_axis=0, tiled=True)
    rows = lax.all_gather(
        at_expert.reshape(experts * capacity, model_width), "z", axis=0, tiled=True
    )
    partial_out = expert_rows(rows, w_in[0], w_out[0])
    expert_sum = lax.psum_scatter(partial_out, "z", scatter_dimension=0, tiled=True)
    summed = lax.all_to_all(
        expert_sum.reshape(experts, capacity, model_width),
        "x",
        split_axis=0,
        concat_axis=0,
        tiled=True,
    ).astype(jnp.float32)
    weighting = placing * gate_rows.T[:, None, :]
    moe_out = jnp.einsum("ect,ecd->td", weighting, summed, precision=lax.Precision.HIGHEST)
    layer_out = (mid_states + moe_out).astype(jnp.bfloat16)
    final_normed = layer_norm(layer_out.astype(jnp.float32), gain_rows[2]).astype(jnp.bfloat16)
    teacher = jax.nn.log_softmax(
        jnp.dot(final_normed, shortlist[0], preferred_element_type=jnp.float32), axis=-1
    )
    learner = jax.nn.log_softmax(student[0], axis=-1)
    picked = (targets[0][:, None] == jnp.arange(student.shape[2])).astype(jnp.float32)
    token_loss = jnp.sum(jnp.exp(teacher) * (teacher - learner), axis=-1) - jnp.sum(
        picked * learner, axis=-1
    )
    counted = jnp.where(decoder, is_valid.astype(jnp.float32), 0.0)
    totals = jnp.stack([jnp.sum(token_loss * counted), jnp.sum(counted)])
    for axis in ("z", "x", "y", "core"):
        totals = lax.psum(totals, axis)
    return (layer_out[None], totals[0] / totals[1])


def solution(mesh):
    segments, expert_devices = mesh.devices.shape
    experts = 4
    fine = Mesh(
        mesh.devices.reshape(segments // 2, 2, experts, expert_devices // experts),
        ("y", "core", "x", "z"),
    )
    seg, exp = (("y", "core"), ("x", "z"))
    placed = (
        P(seg, exp, None),
        P(seg, exp, None),
        P(seg, exp),
        P(seg, exp),
        P(seg, exp, None),
        P(seg, None, None),
        P(seg, None, None),
        P(seg, None, exp),
        P(seg, exp, None),
        P(seg, None, None),
        P(seg, exp, None),
        P(seg, exp),
    )
    return jax.shard_map(
        local, mesh=fine, in_specs=placed, out_specs=(P(seg, exp, None), P()), check_vma=False
    )
```

profile of v0, /device:TPU:1, one launch (start us, length us, event | category | flops | bytes accessed | tf_op | source)
XLA Modules:
  0.0 286.2 jit_solution(16205639869102974398)
XLA Ops:
  7.2 5.8 %collective-permute-start.1 = (bf16[32,2048]{1,0:T(8,128)(2,1)}, bf16[32,2048]{1,0:T(8,128)(2,1)S(1)}, u32[]{:S(2)}, u32[]{:S(2)}) collective-permute-start(bf16[32,2048]{1,0:T(8,128)(2,1)} %bitcast.136), channel_id=1, source_target_pairs={{0,256},{128,384},{1,257},{129,385},{2,258},{130,386},{3,259},{131... | collective-permute-start | bytes 393224 | tf_op jit(solution)/shard_map/ppermute | solution.py:16
  13.7 1.3 collective-permute-start
  15.0 1.0 convert_reduce_fusion
  16.0 0.9 convert_bitcast_fusion
  17.0 0.7 fusion.80
  17.7 1.1 fusion.21
  18.9 0.8 slice_bitcast_fusion.1
  20.5 0.3 fusion.82
  20.8 0.2 fusion.7
  21.4 1.1 fusion.79
  22.5 1.1 multiply_reduce_fusion
  23.6 0.2 fusion.83
  24.0 0.3 convolution_convert_fusion.1
  24.3 10.4 %all_to_all.10 = bf16[4,20,2048]{2,1,0:T(8,128)(2,1)S(1)} all-to-all(bf16[4,20,2048]{2,1,0:T(8,128)(2,1)S(1)} %convolution_convert_fusion.1), channel_id=1, replica_groups=mesh['y'=4,'core'=2,'x'=4,'z'=16] {'x'}, dimensions={0} | all-to-all | bytes 655360 | tf_op jit(solution)/shard_map/all_to_all | solution.py:101
  34.7 0.8 reshape.320
  35.6 76.6 %all-gather.2.cloned.1.call-done = bf16[1280,2048]{1,0:T(8,128)(2,1)} async-done(((bf16[80,2048]{1,0:T(8,128)(2,1)}), bf16[1280,2048]{1,0:T(8,128)(2,1)}) %all-gather.2.cloned.1.call-update) | async-done | bytes 5242896 | tf_op jit(solution)/shard_map/all_gather | solution.py:102
  112.2 10.8 %convolution_convert_fusion = bf16[1280,2048]{1,0:T(8,128)(2,1)} fusion(bf16[1280,2048]{1,0:T(8,128)(2,1)} %all-gather.2.cloned.1.call-done, bf16[1,256,2048]{2,1,0:T(8,128)(2,1)} %param.21, bf16[1,2048,256]{2,1,0:T(8,128)(2,1)} %param.20), kind=kOutput, calls=%fused_computation.1 | convolution fusion | flops 2687631360 | bytes 12582912 | tf_op jit(solution)/shard_map/dot_general | solution.py:29
  123.0 76.6 %reduce-scatter.2.cloned.1.call-done = bf16[80,2048]{1,0:T(8,128)(2,1)} async-done(((bf16[1280,2048]{1,0:T(8,128)(2,1)}), bf16[80,2048]{1,0:T(8,128)(2,1)}) %reduce-scatter.2.cloned.1.call-update) | async-done | bytes 327696 | tf_op jit(solution)/shard_map/reduce_scatter | solution.py:106
  199.5 1.8 reshape.321
  201.3 4.0 %all-to-all-start.1 = ((bf16[4,20,2048]{2,1,0:T(8,128)(2,1)}), bf16[4,20,2048]{2,1,0:T(8,128)(2,1)S(1)}, u32[]{:S(2)}, u32[]{:S(2)}) async-start(bf16[4,20,2048]{2,1,0:T(8,128)(2,1)} %reshape.321), calls=%async_computation.2 | async-start | bytes 786432 | tf_op jit(solution)/shard_map/all_to_all | solution.py:107
  205.7 5.9 %all-to-all-done.1 = bf16[4,20,2048]{2,1,0:T(8,128)(2,1)S(1)} async-done(((bf16[4,20,2048]{2,1,0:T(8,128)(2,1)}), bf16[4,20,2048]{2,1,0:T(8,128)(2,1)S(1)}, u32[]{:S(2)}, u32[]{:S(2)}) %all-to-all-start.1) | async-done | bytes 327712 | tf_op jit(solution)/shard_map/all_to_all | solution.py:107
  211.6 0.5 convert_reduce_fusion.1
  212.2 0.2 fusion.17
  212.4 0.6 fusion.84
  213.2 0.2 select_reduce_fusion.1
  213.4 0.7 multiply_reduce_fusion.2
  214.1 1.3 pad_maximum_fusion
  215.4 21.9 %psum.28 = f32[2]{0:T(128)S(1)} all-reduce(f32[2]{0:T(128)S(1)} %pad_maximum_fusion), channel_id=1, replica_groups=mesh['y'=4,'core'=2,'x'=4,'z'=16] {'z'}, use_global_device_ids=true, to_apply=%region_19.21 | all-reduce | flops 2 | bytes 16 | tf_op jit(solution)/shard_map/psum | solution.py:129
  237.3 6.6 %psum.29 = f32[2]{0:T(128)S(1)} all-reduce(f32[2]{0:T(128)S(1)} %psum.28), channel_id=1, replica_groups=mesh['y'=4,'core'=2,'x'=4,'z'=16] {'x'}, use_global_device_ids=true, to_apply=%region_20.22 | all-reduce | flops 2 | bytes 16 | tf_op jit(solution)/shard_map/psum | solution.py:129
  243.9 8.3 %psum.30 = f32[2]{0:T(128)S(1)} all-reduce(f32[2]{0:T(128)S(1)} %psum.29), channel_id=1, replica_groups=mesh['y'=4,'core'=2,'x'=4,'z'=16] {'y'}, use_global_device_ids=true, to_apply=%region_21.23 | all-reduce | flops 2 | bytes 16 | tf_op jit(solution)/shard_map/psum | solution.py:129
  252.2 24.1 %psum.31 = f32[2]{0:T(128)S(1)} all-reduce(f32[2]{0:T(128)S(1)} %psum.30), channel_id=1, replica_groups=mesh['y'=4,'core'=2,'x'=4,'z'=16] {'core'}, use_global_device_ids=true, to_apply=%region_22.24 | all-reduce | flops 2 | bytes 16 | tf_op jit(solution)/shard_map/psum | solution.py:129
  276.3 0.6 fusion.81
  (41 shorter events, 1.3 us)
Async XLA Ops:
  7.2 205.2 %copy-start = (bf16[1,2048,512]{2,1,0:T(8,128)(2,1)S(1)}, bf16[1,2048,512]{2,1,0:T(8,128)(2,1)}, u32[]{:S(2)}) copy-start(bf16[1,2048,512]{2,1,0:T(8,128)(2,1)} %param.22) | copy-start | bytes 6291460
  7.2 16.5 %copy-start.1 = (bf16[1,32,2048]{2,1,0:T(8,128)(2,1)S(1)}, bf16[1,32,2048]{2,1,0:T(8,128)(2,1)}, u32[]{:S(2)}) copy-start(bf16[1,32,2048]{2,1,0:T(8,128)(2,1)} %param.13) | copy-start | bytes 393220
  7.2 16.4 %copy-start.5 = (bf16[1,2048,4]{1,2,0:T(4,128)(2,1)S(1)}, bf16[1,2048,4]{1,2,0:T(4,128)(2,1)}, u32[]{:S(2)}) copy-start(bf16[1,2048,4]{1,2,0:T(4,128)(2,1)} %param.19) | copy-start | bytes 49156
  7.2 105.0 %all-gather.2.cloned.1.call-start = ((), (), s32[]{:S(2)}) async-start(), calls=%async_computation.3 | async-start | bytes 5570560 | tf_op jit(solution)/shard_map/all_gather | solution.py:102
  7.2 13.2 %collective-permute-start.1 = (bf16[32,2048]{1,0:T(8,128)(2,1)}, bf16[32,2048]{1,0:T(8,128)(2,1)S(1)}, u32[]{:S(2)}, u32[]{:S(2)}) collective-permute-start(bf16[32,2048]{1,0:T(8,128)(2,1)} %bitcast.136), channel_id=1, source_target_pairs={{0,256},{128,384},{1,257},{129,385},{2,258},{130,386},{3,259},{131... | collective-permute-start | bytes 393224 | tf_op jit(solution)/shard_map/ppermute | solution.py:16
  13.7 6.8 %collective-permute-start = (bf16[32]{0:T(256)(128)(2,1)S(1)}, bf16[32]{0:T(256)(128)(2,1)S(1)}, u32[]{:S(2)}, u32[]{:S(2)}) collective-permute-start(bf16[32]{0:T(256)(128)(2,1)S(1)} %compare_convert_fusion.1), channel_id=1, source_target_pairs={{0,256},{128,384},{1,257},{129,385},{2,258},{130,386},{3,259},{131... | collective-permute-start | bytes 200 | tf_op jit(solution)/shard_map/ppermute | solution.py:16
  35.5 164.0 %reduce-scatter.2.cloned.1.call-start = ((), (), s32[]{:S(2)}) async-start(), calls=%async_computation.4 | async-start | bytes 5570560 | tf_op jit(solution)/shard_map/reduce_scatter | solution.py:106
  123.0 82.4 %copy-start.3 = (f32[1,32,512]{2,1,0:T(8,128)S(1)}, f32[1,32,512]{2,1,0:T(8,128)}, u32[]{:S(2)}) copy-start(f32[1,32,512]{2,1,0:T(8,128)} %param.23) | copy-start | bytes 196612
  123.0 90.3 %copy-start.4 = (s32[1,32]{1,0:T(1,128)S(1)}, s32[1,32]{1,0:T(1,128)}, u32[]{:S(2)}) copy-start(s32[1,32]{1,0:T(1,128)} %param.24) | copy-start | bytes 388
  201.3 10.3 %all-to-all-start.1 = ((bf16[4,20,2048]{2,1,0:T(8,128)(2,1)}), bf16[4,20,2048]{2,1,0:T(8,128)(2,1)S(1)}, u32[]{:S(2)}, u32[]{:S(2)}) async-start(bf16[4,20,2048]{2,1,0:T(8,128)(2,1)} %reshape.321), calls=%async_computation.2 | async-start | bytes 786432 | tf_op jit(solution)/shard_map/all_to_all | solution.py:107
  212.1 66.1 %copy-start.2 = (bf16[32,2048]{1,0:T(8,128)(2,1)}, bf16[32,2048]{1,0:T(8,128)(2,1)S(1)}, u32[]{:S(2)}) copy-start(bf16[32,2048]{1,0:T(8,128)(2,1)S(1)} %get-tuple-element.21) | copy-start | bytes 393220
Sparse Core Ops, SparseCore 0:
  35.6 76.4 all-gather.1
  123.1 76.3 reduce-scatter.1
where the time goes:
time: 287 us; the launch traced here: 286 us
  waiting for transfers between devices  159 us (55%)
  blocking collectives  71.2 us (25%)
  between operations  18.1 us (6%)
  matrix products  13.2 us (5%)
  starting transfers between devices  11.2 us (4%)
  other arithmetic  8.34 us (3%)
  local copies, waits for them, and re-layouts  5.08 us (2%)
    all_gather x1, waiting for transfers between devices, local(): lax.all_gather(at_expert.reshape(experts * capacity, model_width), 'z', a...  76.6 us
    reduce_scatter x1, waiting for transfers between devices, local(): lax.psum_scatter(partial_out, 'z', scatter_dimension=0, tiled=True)  76.6 us
    psum x4, blocking collectives, local(): totals = lax.psum(totals, axis)  60.9 us
    dot_general x1, matrix products, expert_rows(): jnp.dot(activated, second_weight, preferred_element_type=jnp.float32)  10.8 us
    all_to_all x1, blocking collectives, local(): lax.all_to_all(buffer, 'x', split_axis=0, concat_axis=0, tiled=True)  10.4 us
    ppermute x2, starting transfers between devices, passed_along(): return lax.ppermute(block, axis, route)  7.08 us
    all_to_all x1, waiting for transfers between devices, local(): lax.all_to_all(expert_sum.reshape(experts, capacity, model_width), 'x', s...  5.91 us
  transfers between devices with their start and end apart: 5, of which 3 were waited for; matrix products, arithmetic and copies ran while one was open for 2% of the time, Pallas kernels for 0%

commit v1 on v0

--- a/solution.py
+++ b/solution.py
@@ -99,8 +99,14 @@
         "ect,td->ecd", placing.astype(jnp.bfloat16), normed, preferred_element_type=jnp.float32
     ).astype(jnp.bfloat16)
     at_expert = lax.all_to_all(buffer, "x", split_axis=0, concat_axis=0, tiled=True)
-    rows = lax.all_gather(
-        at_expert.reshape(experts * capacity, model_width), "z", axis=0, tiled=True
+    rows = jnp.concatenate(
+        lax.all_to_all(
+            jnp.stack([at_expert.reshape(experts * capacity, model_width)] * lax.axis_size("z")),
+            "z",
+            0,
+            0,
+        ),
+        axis=0,
     )
     partial_out = expert_rows(rows, w_in[0], w_out[0])
     expert_sum = lax.psum_scatter(partial_out, "z", scatter_dimension=0, tiled=True)

time: 287 us -> 445 us (1.55)
  blocking collectives: 71.2 us -> 309 us
  waiting for transfers between devices: 159 us -> 79.2 us
    all_to_all x0 -> x1, blocking collectives: none -> 239 us  [local(): lax.all_to_all(jnp.stack([at_expert.reshape(experts * capacity, model_wid...]
    all_gather x1 -> x0, waiting for transfers between devices: 76.6 us -> none  [local(): lax.all_gather(at_expert.reshape(experts * capacity, model_width), 'z', a...]
  transfers between devices with their start and end apart: 5 -> 4, of which waited for: 3 -> 2; matrix products, arithmetic and copies ran while one was open for 2% -> 1% of each run, Pallas kernels for 0% -> 0%
where the time goes in v1:
time: 445 us; the launch traced here: 444 us
  blocking collectives  309 us (69%)
  waiting for transfers between devices  79.2 us (18%)
  between operations  18.1 us (4%)
  matrix products  13.2 us (3%)
  starting transfers between devices  11.1 us (2%)
  other arithmetic  8.34 us (2%)
  local copies, waits for them, and re-layouts  5.01 us (1%)
    all_to_all x1, blocking collectives, local(): lax.all_to_all(jnp.stack([at_expert.reshape(experts * capacity, model_wid...  239 us
    reduce_scatter x1, waiting for transfers between devices, local(): lax.psum_scatter(partial_out, 'z', scatter_dimension=0, tiled=True)  73.2 us
    psum x4, blocking collectives, local(): totals = lax.psum(totals, axis)  60.4 us
    dot_general x1, matrix products, expert_rows(): jnp.dot(activated, second_weight, preferred_element_type=jnp.float32)  10.7 us
    all_to_all x1, blocking collectives, local(): lax.all_to_all(buffer, 'x', split_axis=0, concat_axis=0, tiled=True)  10.4 us
  transfers between devices with their start and end apart: 4, of which 2 were waited for; matrix products, arithmetic and copies ran while one was open for 1% of the time, Pallas kernels for 0%

profile of v1, /device:TPU:1, one launch (start us, length us, event | category | flops | bytes accessed | tf_op | source)
XLA Modules:
  0.0 444.4 jit_solution(532816589148125224)
XLA Ops:
  7.2 5.8 %collective-permute-start.1 = (bf16[32,2048]{1,0:T(8,128)(2,1)}, bf16[32,2048]{1,0:T(8,128)(2,1)S(1)}, u32[]{:S(2)}, u32[]{:S(2)}) collective-permute-start(bf16[32,2048]{1,0:T(8,128)(2,1)} %bitcast.138), channel_id=1, source_target_pairs={{0,256},{128,384},{1,257},{129,385},{2,258},{130,386},{3,259},{131... | collective-permute-start | bytes 393224 | tf_op jit(solution)/shard_map/ppermute | solution.py:16
  13.7 1.3 collective-permute-start
  15.0 1.0 convert_reduce_fusion
  16.0 0.9 convert_bitcast_fusion
  17.0 0.7 fusion.80
  17.7 1.1 fusion.21
  18.9 0.8 slice_bitcast_fusion.1
  20.5 0.3 fusion.82
  20.8 0.2 fusion.7
  21.4 1.1 fusion.79
  22.5 1.1 multiply_reduce_fusion
  23.6 0.2 fusion.83
  24.0 0.3 convolution_convert_fusion.1
  24.3 10.4 %all_to_all.15 = bf16[4,20,2048]{2,1,0:T(8,128)(2,1)S(1)} all-to-all(bf16[4,20,2048]{2,1,0:T(8,128)(2,1)S(1)} %convolution_convert_fusion.1), channel_id=1, replica_groups=mesh['y'=4,'core'=2,'x'=4,'z'=16] {'x'}, dimensions={0} | all-to-all | bytes 655360 | tf_op jit(solution)/shard_map/all_to_all | solution.py:101
  34.8 0.6 stack.12
  35.4 238.7 %all_to_all.16 = bf16[16,80,2048]{2,1,0:T(8,128)(2,1)} all-to-all(bf16[16,80,2048]{2,1,0:T(8,128)(2,1)S(1)} %stack.12), channel_id=1, replica_groups=mesh['y'=4,'core'=2,'x'=4,'z'=16] {'z'}, dimensions={0} | all-to-all | bytes 10485760 | tf_op jit(solution)/shard_map/all_to_all | solution.py:103
  274.2 10.7 %convolution_convert_fusion = bf16[1280,2048]{1,0:T(8,128)(2,1)} fusion(bf16[1280,2048]{1,0:T(8,128)(2,1)} %bitcast.128, bf16[1,256,2048]{2,1,0:T(8,128)(2,1)} %param.21, bf16[1,2048,256]{2,1,0:T(8,128)(2,1)} %param.20), kind=kOutput, calls=%fused_computation.1 | convolution fusion | flops 2687631360 | bytes 12582912 | tf_op jit(solution)/shard_map/dot_general | solution.py:29
  284.9 73.2 %reduce-scatter.2.cloned.1.call-done = bf16[80,2048]{1,0:T(8,128)(2,1)} async-done(((bf16[1280,2048]{1,0:T(8,128)(2,1)}), bf16[80,2048]{1,0:T(8,128)(2,1)}) %reduce-scatter.2.cloned.1.call-update) | async-done | bytes 327696 | tf_op jit(solution)/shard_map/reduce_scatter | solution.py:112
  358.2 1.8 reshape.323
  360.0 4.0 all-to-all-start.2
  364.3 5.9 %all-to-all-done.2 = bf16[4,20,2048]{2,1,0:T(8,128)(2,1)S(1)} async-done(((bf16[4,20,2048]{2,1,0:T(8,128)(2,1)}), bf16[4,20,2048]{2,1,0:T(8,128)(2,1)S(1)}, u32[]{:S(2)}, u32[]{:S(2)}) %all-to-all-start.2) | async-done | bytes 327712 | tf_op jit(solution)/shard_map/all_to_all | solution.py:113
  370.2 0.5 convert_reduce_fusion.1
  370.8 0.2 fusion.17
  371.0 0.6 fusion.84
  371.8 0.2 select_reduce_fusion.1
  372.0 0.7 multiply_reduce_fusion.2
  372.7 1.3 pad_maximum_fusion
  374.0 21.3 %psum.28 = f32[2]{0:T(128)S(1)} all-reduce(f32[2]{0:T(128)S(1)} %pad_maximum_fusion), channel_id=1, replica_groups=mesh['y'=4,'core'=2,'x'=4,'z'=16] {'z'}, use_global_device_ids=true, to_apply=%region_19.21 | all-reduce | flops 2 | bytes 16 | tf_op jit(solution)/shard_map/psum | solution.py:135
  395.3 6.9 %psum.29 = f32[2]{0:T(128)S(1)} all-reduce(f32[2]{0:T(128)S(1)} %psum.28), channel_id=1, replica_groups=mesh['y'=4,'core'=2,'x'=4,'z'=16] {'x'}, use_global_device_ids=true, to_apply=%region_20.22 | all-reduce | flops 2 | bytes 16 | tf_op jit(solution)/shard_map/psum | solution.py:135
  402.2 8.7 %psum.30 = f32[2]{0:T(128)S(1)} all-reduce(f32[2]{0:T(128)S(1)} %psum.29), channel_id=1, replica_groups=mesh['y'=4,'core'=2,'x'=4,'z'=16] {'y'}, use_global_device_ids=true, to_apply=%region_21.23 | all-reduce | flops 2 | bytes 16 | tf_op jit(solution)/shard_map/psum | solution.py:135
  410.9 23.5 %psum.31 = f32[2]{0:T(128)S(1)} all-reduce(f32[2]{0:T(128)S(1)} %psum.30), channel_id=1, replica_groups=mesh['y'=4,'core'=2,'x'=4,'z'=16] {'core'}, use_global_device_ids=true, to_apply=%region_22.24 | all-reduce | flops 2 | bytes 16 | tf_op jit(solution)/shard_map/psum | solution.py:135
  434.4 0.6 fusion.81
  (40 shorter events, 1.3 us)
Async XLA Ops:
  7.2 363.8 %copy-start = (bf16[1,2048,512]{2,1,0:T(8,128)(2,1)S(1)}, bf16[1,2048,512]{2,1,0:T(8,128)(2,1)}, u32[]{:S(2)}) copy-start(bf16[1,2048,512]{2,1,0:T(8,128)(2,1)} %param.22) | copy-start | bytes 6291460
  7.2 16.5 %copy-start.1 = (bf16[1,32,2048]{2,1,0:T(8,128)(2,1)S(1)}, bf16[1,32,2048]{2,1,0:T(8,128)(2,1)}, u32[]{:S(2)}) copy-start(bf16[1,32,2048]{2,1,0:T(8,128)(2,1)} %param.13) | copy-start | bytes 393220
  7.2 16.4 %copy-start.5 = (bf16[1,2048,4]{1,2,0:T(4,128)(2,1)S(1)}, bf16[1,2048,4]{1,2,0:T(4,128)(2,1)}, u32[]{:S(2)}) copy-start(bf16[1,2048,4]{1,2,0:T(4,128)(2,1)} %param.19) | copy-start | bytes 49156
  7.2 351.0 %reduce-scatter.2.cloned.1.call-start = ((), (), s32[]{:S(2)}) async-start(), calls=%async_computation.4 | async-start | bytes 5570560 | tf_op jit(solution)/shard_map/reduce_scatter | solution.py:112
  7.2 13.2 %collective-permute-start.1 = (bf16[32,2048]{1,0:T(8,128)(2,1)}, bf16[32,2048]{1,0:T(8,128)(2,1)S(1)}, u32[]{:S(2)}, u32[]{:S(2)}) collective-permute-start(bf16[32,2048]{1,0:T(8,128)(2,1)} %bitcast.138), channel_id=1, source_target_pairs={{0,256},{128,384},{1,257},{129,385},{2,258},{130,386},{3,259},{131... | collective-permute-start | bytes 393224 | tf_op jit(solution)/shard_map/ppermute | solution.py:16
  13.7 6.8 %collective-permute-start = (bf16[32]{0:T(256)(128)(2,1)S(1)}, bf16[32]{0:T(256)(128)(2,1)S(1)}, u32[]{:S(2)}, u32[]{:S(2)}) collective-permute-start(bf16[32]{0:T(256)(128)(2,1)S(1)} %compare_convert_fusion.1), channel_id=1, source_target_pairs={{0,256},{128,384},{1,257},{129,385},{2,258},{130,386},{3,259},{131... | collective-permute-start | bytes 200 | tf_op jit(solution)/shard_map/ppermute | solution.py:16
  284.9 79.0 %copy-start.3 = (f32[1,32,512]{2,1,0:T(8,128)S(1)}, f32[1,32,512]{2,1,0:T(8,128)}, u32[]{:S(2)}) copy-start(f32[1,32,512]{2,1,0:T(8,128)} %param.23) | copy-start | bytes 196612
  284.9 86.9 %copy-start.4 = (s32[1,32]{1,0:T(1,128)S(1)}, s32[1,32]{1,0:T(1,128)}, u32[]{:S(2)}) copy-start(s32[1,32]{1,0:T(1,128)} %param.24) | copy-start | bytes 388
  360.0 10.2 %all-to-all-start.2 = ((bf16[4,20,2048]{2,1,0:T(8,128)(2,1)}), bf16[4,20,2048]{2,1,0:T(8,128)(2,1)S(1)}, u32[]{:S(2)}, u32[]{:S(2)}) async-start(bf16[4,20,2048]{2,1,0:T(8,128)(2,1)} %reshape.323), calls=%async_computation.3 | async-start | bytes 786432 | tf_op jit(solution)/shard_map/all_to_all | solution.py:113
  370.7 65.6 %copy-start.2 = (bf16[32,2048]{1,0:T(8,128)(2,1)}, bf16[32,2048]{1,0:T(8,128)(2,1)S(1)}, u32[]{:S(2)}) copy-start(bf16[32,2048]{1,0:T(8,128)(2,1)S(1)} %get-tuple-element.21) | copy-start | bytes 393220
Sparse Core Ops, SparseCore 0:
  285.1 73.0 reduce-scatter.1
